TPU v7x, 128 devices: a whole 4x4x4 slice. The times are simulated.
128 devices in a mesh: lat: 16 (over y, x), lon: 8 (over z, core).
Axes of the slice: x: 4, y: 4, z: 4, core: 2. Of those that a mesh axis runs over, the one named last changes fastest.
Arguments:
- state_start: float32 [6, 2048, 7200], P(None, 'lat', 'lon'), may hold values from -6 to 6
- state_section: float32 [6, 2048, 7200], P(None, 'lat', 'lon'), may hold values from -6 to 6
- zonal_courant: float32 [6, 2048, 7200], P(None, 'lat', 'lon'), may hold values from -0.4 to 0.4
- merid_courant: float32 [6, 2048, 7200], P(None, 'lat', 'lon'), may hold values from -0.4 to 0.4
- cutoffs: int32 [2048], replicated, may hold values from 64 to 511, as said below
- nest_values: float32 [2, 6, 128, 256], P(None, None, ('lat', 'lon')), may hold values from -6 to 6
- nest_corners: int32 [2, 2], replicated, may hold values from 0 to 6944, as said below
Outputs:
- new_state: float32 [6, 2048, 7200], P(None, 'lat', 'lon')
Inputs may be any that keep to these rules, and one draw needn't show every extreme that they name: `cutoffs`: only rows poleward of 45 degrees are read; among them the value 512 - 1 occurs in a southern row and 64 in a northern row. `nest_corners`: block 0 lies wholly in the southern half of the rows, block 1 wholly in the northern half; each block lies inside the grid without crossing the longitude seam; one entry always equals the stated most.
All inputs are finite; a program needn't handle non-finite values.
Results may differ from a plain program's by a relative error of at most 0.000067.
Values sent between devices are 32-bit elements; how exact they have to be, the bound alone decides.
A program may use at most 128 MiB of HBM per device.

v0:
```python
import math

import jax
import jax.numpy as jnp
import ml_dtypes
import numpy as np
from jax import lax
from jax.experimental import pallas as pl
from jax.experimental.pallas import tpu as pltpu
from jax.sharding import PartitionSpec as P

LEV, NLAT, NLON, KMAX = 6, 2048, 7200, 512
BANDS, SEGS = 16, 8
ROWS, SEG = NLAT // BANDS, NLON // SEGS
RANK = 160
PART = RANK // 4
CHUNKS, PAIR = 3, 2
STEP, STEPS = 32, 29
TALL = STEP * STEPS + 8
WIDE = 1024
MESH = pl.DeviceIdType.MESH
BF = ml_dtypes.bfloat16


def tri_solve(diag, off, shift, rhs):
    n, r = rhs.shape
    b = rhs.copy()
    d, u1, u2 = (np.zeros((n, r)) for _ in range(3))
    cd, cu, cb = diag[0] - shift, np.full(r, off[0]), b[0]
    for j in range(n - 1):
        nd, nu, sub = diag[j + 1] - shift, off[j + 1] if j + 2 < n else 0.0, off[j]
        swap = np.abs(sub) > np.abs(cd)
        p = np.where(swap, sub, np.where(cd == 0, 1e-30, cd))
        pu1, pu2, pb = np.where(swap, nd, cu), np.where(swap, nu, 0.0), np.where(swap, b[j + 1], cb)
        o, ou1 = np.where(swap, cd, sub), np.where(swap, cu, nd)
        ou2, ob = np.where(swap, 0.0, nu), np.where(swap, cb, b[j + 1])
        f = o / p
        d[j], u1[j], u2[j], b[j] = p, pu1, pu2, pb
        cd, cu, cb = ou1 - f * pu1, ou2 - f * pu2, ob - f * pb
    d[n - 1] = np.where(np.abs(cd) < 1e-20, 1e-20, cd)
    b[n - 1] = cb
    x = np.zeros((n, r))
    x[n - 1] = b[n - 1] / d[n - 1]
    x[n - 2] = (b[n - 2] - u1[n - 2] * x[n - 1]) / d[n - 2]
    for j in range(n - 3, -1, -1):
        x[j] = (b[j] - u1[j] * x[j + 1] - u2[j] * x[j + 2]) / d[j]
    return x


def slepian(length, width, rank):
    i = np.arange(length, dtype=np.float64)
    diag = ((length - 1 - 2 * i) / 2) ** 2 * np.cos(2 * np.pi * width)
    off = (i * (length - i) / 2)[1:]
    off2 = np.concatenate([[0.0], off**2])
    bound = np.abs(diag).max() + 2 * off.max()
    low, high, want = np.full(rank, -bound), np.full(rank, bound), np.arange(rank)
    for _ in range(70):
        mid = 0.5 * (low + high)
        above, q = np.zeros(rank, dtype=np.int64), np.ones(rank)
        for j in range(length):
            q = diag[j] - mid - off2[j] / q
            q = np.where(q == 0.0, 1e-300, q)
            above += q > 0
        up = above > want
        low, high = np.where(up, mid, low), np.where(up, high, mid)
    x = np.ones((length, rank)) + 0.3 * np.cos(i * i)[:, None]
    for _ in range(4):
        x = tri_solve(diag, off, 0.5 * (low + high), x)
        x = x / np.sqrt((x * x).sum(0))
    return x


def split(x):
    hi = x.astype(BF)
    return hi, (x - hi.astype(np.float64)).astype(BF)


def make_tables():
    basis = slepian(SEG, 512.0 / NLON, RANK)
    k, i = np.arange(KMAX), np.arange(SEG)
    waves = np.exp(-2j * np.pi * ((i[:, None] * k[None, :]) % NLON) / NLON)
    v = np.einsum("ir,ik->rk", basis, waves)
    weight = np.where(k == 0, 1.0, 2.0) / NLON
    uh, ul = split(basis)
    ut = np.zeros((2 * RANK, WIDE), BF)
    ut[:RANK, :SEG], ut[RANK:, :SEG] = uh.T, ul.T
    eu = np.zeros((STEP * STEPS, 512), BF)
    eu[:SEG, :RANK], eu[:SEG, RANK : 2 * RANK], eu[:SEG, 2 * RANK : 3 * RANK] = uh, uh, ul
    pt = np.zeros((4, 256, WIDE), BF)
    qt = np.zeros((4, 2 * RANK, 768), BF)
    for g in range(4):
        s1, s2 = g, (4 if g == 0 else 8 - g)
        k1, k2 = np.arange(64) * 8 + s1, np.arange(64) * 8 + s2
        v1, v2 = v[:, k1], v[:, k2]
        w1, w2 = weight[k1], weight[k2]
        z = np.zeros((RANK, 64))
        if g == 0:
            p = np.block([[v1.real, z, v1.imag, z], [z, v2.real, z, v2.imag]])
            q = np.block([[v1.real * w1, z, v1.imag * w1, z], [z, v2.real * w2, z, v2.imag * w2]])
        else:
            p = np.block([[v1.real, v2.real, v1.imag, v2.imag], [-v1.imag, v2.imag, v1.real, -v2.real]])
            q = np.block(
                [
                    [v1.real * w1, v2.real * w2, v1.imag * w1, v2.imag * w2],
                    [-v1.imag * w1, v2.imag * w2, v1.real * w1, -v2.real * w2],
                ]
            )
        ph, pl_ = split(p.T)
        pt[g, :, :320], pt[g, :, 320:640], pt[g, :, 640:960] = ph, ph, pl_
        qh, ql = split(q)
        qt[g, :, :256], qt[g, :, 256:512], qt[g, :, 512:] = qh, qh, ql
    step = np.float32(math.pi / NLAT)
    half = np.float32(math.pi / 2)
    e = np.arange(NLAT + 1)
    edge = np.cos((e.astype(np.float32) * step - half).astype(np.float64)).astype(np.float32)
    edge[0] = edge[-1] = 0.0
    center = np.cos(((np.arange(NLAT).astype(np.float32) + np.float32(0.5)) * step - half).astype(np.float64))
    rc = np.zeros((BANDS, 8, ROWS), np.float32)
    for b in range(BANDS):
        r0 = b * ROWS
        rc[b, 0] = 0.0625 * edge[r0 + 1 : r0 + ROWS + 1]
        rc[b, 1] = (1.0 / center[r0 : r0 + ROWS]).astype(np.float32)
        rc[b, 2] = 0.0625 * edge[r0]
        rc[b, 3] = 0.0625 * edge[r0 + ROWS]
    return ut, eu, pt, qt, rc


def lanes(shape):
    return lax.broadcasted_iota(jnp.int32, shape, len(shape) - 1)


def hi_lo(x):
    hi = x.astype(jnp.bfloat16)
    return hi, (x - hi.astype(jnp.float32)).astype(jnp.bfloat16)


def dot(a, b):
    return jnp.dot(a, b, preferred_element_type=jnp.float32)


def section_kernel(
    start, sec, zon, mer, ut_h, pt_h, qt_h, cut, rc, nest,
    zout, sect, nestg,
    sb, tb, zb, mb, ut, pt, qt, sh, sl, pk, pkr, fl, lh,
    fsend, recv, bsend, nsend, ngat, nasm,
    ld, tabs, psend, precv, lsend, lrecv, fs, fr, bs, br, n1s, n1r, n2s, n2r, osem, zsem,
):
    lat, lon = lax.axis_index("lat"), lax.axis_index("lon")
    polar = (lat < BANDS // 4) | (lat >= BANDS - BANDS // 4)

    loads = []
    for c in range(CHUNKS):
        pair = pl.ds(PAIR * c, PAIR)
        loads.append([])
        for a, (src, dst) in enumerate(((sec, tb), (mer, mb), (zon, zb), (start, sb))):
            copy = pltpu.make_async_copy(src.at[pair], dst.at[pair, pl.ds(0, SEG)], ld.at[c, a])
            copy.start()
            loads[c].append(copy)
    tables = [
        pltpu.make_async_copy(src, dst, tabs.at[n]) for n, (src, dst) in enumerate(((ut_h, ut), (pt_h, pt), (qt_h, qt)))
    ]
    for copy in tables:
        copy.start()

    barrier = pltpu.get_barrier_semaphore()
    for k in range(1, SEGS):
        pl.semaphore_signal(barrier, inc=1, device_id=(lat, lax.rem(lon + k, SEGS)), device_id_type=MESH)
    for k in range(1, BANDS):
        pl.semaphore_signal(barrier, inc=1, device_id=(lax.rem(lat + k, BANDS), lon), device_id_type=MESH)
    for n in range(12):
        nsend[n : n + 1, :] = nest[n // 6, n % 6]
    nsend[12:16, :] = jnp.zeros((4, 256), jnp.float32)
    for buf in (tb, zb, mb, sb):
        for lev in range(LEV):
            buf[lev, SEG:TALL, :] = jnp.zeros((TALL - SEG, ROWS), jnp.float32)
    sh[STEP * STEPS :, :] = jnp.zeros((WIDE - STEP * STEPS, 256), jnp.bfloat16)
    sl[STEP * STEPS :, :] = jnp.zeros((WIDE - STEP * STEPS, 256), jnp.bfloat16)
    pl.semaphore_wait(barrier, SEGS - 1 + BANDS - 1)

    left, right = lax.rem(lon + SEGS - 1, SEGS), lax.rem(lon + 1, SEGS)
    lon_copies = []
    for a, src in enumerate((sec, zon)):
        for way, (row, to) in enumerate(((0, left), (SEG - 1, right))):
            copy = pltpu.make_async_remote_copy(
                src_ref=src.at[:, pl.ds(row, 1), :], dst_ref=lh.at[a, way], send_sem=lsend.at[a, way],
                recv_sem=lrecv.at[a, way], device_id=(lat, to), device_id_type=MESH,
            )
            copy.start()
            lon_copies.append(copy)
    nest_copies = []
    for k in range(1, SEGS):
        copy = pltpu.make_async_remote_copy(
            src_ref=nsend, dst_ref=ngat.at[lon], send_sem=n1s.at[k], recv_sem=n1r.at[k],
            device_id=(lat, lax.rem(lon + k, SEGS)), device_id_type=MESH,
        )
        copy.start()
        nest_copies.append(copy)
    ngat[lon] = nsend[...]

    before, after = lax.rem(lat + BANDS - 1, BANDS), lax.rem(lat + 1, BANDS)
    lane = lanes((STEP, ROWS))
    even = (lane & 1) == 0
    lat_copies = []
    for c in range(CHUNKS):
        loads[c][0].wait()
        loads[c][1].wait()

        def pack(b, acc, c=c):
            out = []
            for buf, x in zip((tb, mb), acc):
                for h in range(PAIR):
                    v = buf[PAIR * c + h, pl.ds(pl.multiple_of(b * STEP, STEP), STEP), :]
                    x = jnp.where((lane >> 1) == 2 * b + h, pltpu.roll(v, lax.rem(4 * b + 2 * h + 1, ROWS), 1), x)
                out.append(x)
            return tuple(out)

        none = jnp.zeros((STEP, ROWS), jnp.float32)
        packed = lax.fori_loop(0, STEPS, pack, (none, none))
        for a in range(2):
            pk[c, a] = packed[a]
        for way, to in enumerate((after, before)):
            copy = pltpu.make_async_remote_copy(
                src_ref=pk.at[c], dst_ref=pkr.at[c, way], send_sem=psend.at[c, way], recv_sem=precv.at[c, way],
                device_id=(to, lon), device_id_type=MESH,
            )
            copy.start()
            lat_copies.append(copy)

    for copy in nest_copies:
        copy.wait_recv()
    for n in range(12):
        nasm[n // 6, n % 6] = jnp.concatenate([ngat[d, n : n + 1, :] for d in range(SEGS)], axis=0)
    spread = []
    eight = pl.ds(pl.multiple_of(lat * SEGS, SEGS), SEGS)
    for k in range(1, BANDS):
        to = lax.rem(lat + k, BANDS)
        copy = pltpu.make_async_remote_copy(
            src_ref=nasm.at[to // (BANDS // 2)], dst_ref=nestg.at[:, eight, :], send_sem=n2s.at[k],
            recv_sem=n2r.at[k], device_id=(to, lon), device_id_type=MESH,
        )
        copy.start()
        spread.append(copy)
    own_nest = pltpu.make_async_copy(nasm.at[lat // (BANDS // 2)], nestg.at[:, eight, :], osem.at[LEV])
    own_nest.start()

    for copy in lon_copies:
        copy.wait_recv()
    edge_row = rc[lat, 0:1, :]
    inverse_cos = rc[lat, 1:2, :]
    first_edge, last_edge = rc[lat, 2:3, :], rc[lat, 3:4, :]
    flux_scale = jnp.where(even[:1], last_edge, first_edge)

    def fluxes(c, put):
        for copy in loads[c][2:]:
            copy.wait()
        for way in range(2):
            lat_copies[2 * c + way].wait_recv()
        sums = [
            pk[c, a] + jnp.where(even, pltpu.roll(pkr[c, 1, a], ROWS - 1, 1), pltpu.roll(pkr[c, 0, a], 1, 1))
            for a in range(2)
        ]
        fl[c] = sums[0] * sums[1] * flux_scale
        for h in range(PAIR):
            lev = PAIR * c + h
            tb[lev, SEG : SEG + 1, :] = lh[0, 0, lev]
            zb[lev, SEG : SEG + 1, :] = lh[1, 0, lev]
            west = 0.0625 * (lh[1, 1, lev] + zb[lev, 0:1, :]) * (lh[0, 1, lev] + tb[lev, 0:1, :])

            def step(b, west, lev=lev, h=h):
                r = pl.multiple_of(b * STEP, STEP)
                t_all = tb[lev, pl.ds(r, STEP + 8), :]
                z_all = zb[lev, pl.ds(r, STEP + 8), :]
                t = t_all[:STEP]
                east = 0.0625 * (z_all[:STEP] + z_all[1 : STEP + 1]) * (t + t_all[1 : STEP + 1])
                zonal = east - jnp.concatenate([west, east[: STEP - 1]], axis=0)
                m = mb[lev, pl.ds(r, STEP), :]
                ends = pltpu.roll(fl[c], lax.rem(2 * ROWS - 1 - 4 * b - 2 * h, ROWS), 1)
                south = edge_row * (t + pltpu.roll(t, ROWS - 1, 1)) * (m + pltpu.roll(m, ROWS - 1, 1))
                south = jnp.where(lane == ROWS - 1, ends, south)
                north = jnp.where(lane == 0, ends, pltpu.roll(south, 1, 1))
                s = sb[lev, pl.ds(r, STEP), :]
                put(lev, h, r, 0.75 * s + 0.25 * t - zonal - inverse_cos * (south - north))
                return east[STEP - 1 : STEP]

            lax.fori_loop(0, STEPS, step, west)

    @pl.when(jnp.logical_not(polar))
    def _():
        def put(lev, h, r, value):
            sb[lev, pl.ds(r, STEP), :] = value

        outs = []
        for c in range(CHUNKS):
            fluxes(c, put)
            pair = pl.ds(PAIR * c, PAIR)
            copy = pltpu.make_async_copy(sb.at[pair, pl.ds(0, SEG)], sect.at[pair], osem.at[c])
            copy.start()
            outs.append(copy)
        for copy in outs:
            copy.wait()
        for copy in tables:
            copy.wait()

    @pl.when(polar)
    def _():
        def put(lev, h, r, value):
            hi, lo = hi_lo(value)
            sh[pl.ds(r, STEP), h * ROWS : (h + 1) * ROWS] = hi
            sl[pl.ds(r, STEP), h * ROWS : (h + 1) * ROWS] = lo

        block = lanes((PART, ROWS)) // 32

        def exchange(c, k, src, dst, send, receive):
            return pltpu.make_async_remote_copy(
                src_ref=src.at[c, lax.rem(lon + k, SEGS)], dst_ref=dst.at[c, lon], send_sem=send.at[c, k],
                recv_sem=receive.at[c, k], device_id=(lat, lax.rem(lon + k, SEGS)), device_id_type=MESH,
            )

        there = []
        for c in range(CHUNKS):
            fluxes(c, put)
            if c == 0:
                tables[0].wait()
            both = dot(ut[...], sh[...])
            y = both[:RANK] + both[RANK:] + dot(ut[:RANK, :], sl[...])
            for h in range(PAIR):
                for q in range(4):
                    acc = None
                    for j in range(4):
                        v = y[PART * j : PART * (j + 1), ROWS * h : ROWS * (h + 1)]
                        if j != q:
                            v = pltpu.roll(v, (32 * (j - q)) % ROWS, 1)
                        acc = v if acc is None else jnp.where(block == j, v, acc)
                    fsend[c, 4 * h + q] = acc
            recv[c, lon] = fsend[c, lon]
            there.append([exchange(c, k, fsend, recv, fs, fr) for k in range(1, SEGS)])
            for copy in there[c]:
                copy.start()

        tables[1].wait()
        tables[2].wait()
        rows_cut = pltpu.roll(jnp.broadcast_to(cut[pl.ds(lat, 1), :], (8, ROWS)), ROWS - 32 * lax.rem(lon, 4), 1)[:1]
        n = lax.broadcasted_iota(jnp.int32, (256, ROWS), 0)
        root = math.sqrt(0.5)
        back, own = [], []
        for c in range(CHUNKS):
            for copy in there[c]:
                copy.wait_recv()
            y = [recv[c, d] for d in range(SEGS)]
            u = [y[j] + y[j + 4] for j in range(4)]
            v = [y[j] - y[j + 4] for j in range(4)]
            a, b, m, p = u[0] + u[2], u[1] + u[3], root * (v[1] - v[3]), root * (v[1] + v[3])
            groups = [(a + b, a - b), (v[0] + m, -v[2] - p), (u[0] - u[2], u[3] - u[1]), (v[0] - m, v[2] - p)]
            spectra = []
            for g, two in enumerate(groups):
                tall = jnp.concatenate(
                    [x if j == 0 else pltpu.roll(x, ROWS - 32 * j, 1) for x in two for j in range(4)], axis=0
                )
                hi, lo = hi_lo(tall)
                rhs = jnp.concatenate([hi, lo, hi, jnp.zeros((WIDE - 960, ROWS), jnp.bfloat16)], axis=0)
                wave = dot(pt[g], rhs)
                number = 8 * (n & 63) + jnp.where((n & 64) == 0, g, 4 if g == 0 else 8 - g)
                wave = jnp.where(number <= rows_cut, wave, 0.0)
                hi, lo = hi_lo(wave)
                full = dot(qt[g], jnp.concatenate([hi, lo, hi], axis=0))
                for x in range(2):
                    acc = None
                    for j in range(4):
                        w = full[RANK * x + PART * j : RANK * x + PART * (j + 1)]
                        if j:
                            w = pltpu.roll(w, 32 * j, 1)
                        acc = w if acc is None else jnp.where(block == j, w, acc)
                    spectra.append(acc)
            w0, w4, r1, i1, r2, i2, r3, i3 = spectra
            plus, minus = w0 + w4, w0 - w4
            evens = [plus + r2, minus - i2, plus - r2, minus + i2]
            d1, d2 = root * (r1 - r3), root * (i1 + i3)
            odds = [r1 + r3, d1 - d2, i3 - i1, -d1 - d2]
            for e in range(4):
                bsend[c, e] = evens[e] + odds[e]
                bsend[c, e + 4] = evens[e] - odds[e]
            back.append([exchange(c, k, bsend, zout, bs, br) for k in range(1, SEGS)])
            for copy in back[c]:
                copy.start()
            copy = pltpu.make_async_copy(bsend.at[c, lon], zout.at[c, lon], zsem.at[c])
            copy.start()
            own.append(copy)
        for c in range(CHUNKS):
            own[c].wait()
            for copy in back[c]:
                copy.wait_recv()
        for c in range(CHUNKS):
            for copy in there[c] + back[c]:
                copy.wait_send()

    for copy in spread:
        copy.wait_recv()
    own_nest.wait()
    for copy in lon_copies + nest_copies + lat_copies + spread:
        copy.wait_send()


def finish_kernel(lat_ref, corners, zin, eu, sect, nestg, out, ob, nb, zc, osem, nsem):
    lat, lon = lat_ref[0], lat_ref[1]
    polar = (lat < BANDS // 4) | (lat >= BANDS - BANDS // 4)
    half = lat // (BANDS // 2)
    row = corners[half, 0] - lat * ROWS
    col = corners[half, 1] - lon * SEG
    hit = (row > -ROWS) & (row < ROWS) & (col > -256) & (col < SEG)
    fetch = pltpu.make_async_copy(nestg, nb, nsem)

    @pl.when(hit)
    def _():
        fetch.start()

    @pl.when(jnp.logical_not(polar))
    def _():
        copy = pltpu.make_async_copy(sect, ob.at[:, pl.ds(256, SEG), :], osem.at[0])
        copy.start()
        copy.wait()

    block = lanes((PART, ROWS)) // 32

    @pl.when(polar)
    def _():
        for c in range(CHUNKS):
            for h in range(PAIR):
                for j in range(4):
                    acc = None
                    for q in range(4):
                        v = zin[c, 4 * h + q]
                        if j != q:
                            v = pltpu.roll(v, (32 * (q - j)) % ROWS, 1)
                        acc = v if acc is None else jnp.where(block == q, v, acc)
                    zc[PART * j : PART * (j + 1), h * ROWS : (h + 1) * ROWS] = acc
            hi, lo = hi_lo(zc[...])
            rhs = jnp.concatenate([hi, lo, hi, jnp.zeros((32, 2 * ROWS), jnp.bfloat16)], axis=0)
            full = dot(eu[...], rhs)
            for h in range(PAIR):
                ob[PAIR * c + h, 256 : 256 + STEP * STEPS, :] = full[:, h * ROWS : (h + 1) * ROWS]

    @pl.when(hit)
    def _():
        fetch.wait()
        lane = lanes((264, ROWS))
        cell = lax.broadcasted_iota(jnp.int32, (264, ROWS), 0)
        place = col + 256
        base = pl.multiple_of((place // 8) * 8, 8)
        off = place - base
        inside = (lane >= row) & (lane < row + ROWS) & (cell >= off) & (cell < off + 256)
        for lev in range(LEV):
            flat = jnp.swapaxes(nb[lev], 0, 1)
            tall = jnp.concatenate([flat, jnp.zeros((8, ROWS), jnp.float32)], axis=0)
            tall = pltpu.roll(pltpu.roll(tall, off, 0), lax.rem(row + ROWS, ROWS), 1)
            here = ob[lev, pl.ds(base, 264), :]
            ob[lev, pl.ds(base, 264), :] = jnp.where(inside, tall, here)

    copies = []
    for lev in range(LEV):
        copy = pltpu.make_async_copy(ob.at[lev, pl.ds(256, SEG), :], out.at[lev], osem.at[lev])
        copy.start()
        copies.append(copy)
    for copy in copies:
        copy.wait()


def shards(start, sec, zon, mer, cutoffs, nest_values, nest_corners, tables):
    ut, eu, pt, qt, rc = (jnp.asarray(x) for x in tables)
    flip = lambda x: jnp.swapaxes(x, 1, 2)
    anywhere = pl.BlockSpec(memory_space=pl.ANY)
    vmem = pl.BlockSpec(memory_space=pltpu.VMEM)
    smem = pl.BlockSpec(memory_space=pltpu.SMEM)
    f32, bf = jnp.float32, jnp.bfloat16
    dma = pltpu.SemaphoreType.DMA
    field = pltpu.VMEM((LEV, TALL, ROWS), f32)
    zout, sect, nestg = pl.pallas_call(
        section_kernel,
        out_shape=(
            jax.ShapeDtypeStruct((CHUNKS, SEGS, PART, ROWS), f32),
            jax.ShapeDtypeStruct((LEV, SEG, ROWS), f32),
            jax.ShapeDtypeStruct((LEV, 128, 256), f32),
        ),
        in_specs=[anywhere] * 7 + [vmem] * 3,
        out_specs=(anywhere,) * 3,
        scratch_shapes=[
            field, field, field, field,
            pltpu.VMEM((2 * RANK, WIDE), bf), pltpu.VMEM((4, 256, WIDE), bf), pltpu.VMEM((4, 2 * RANK, 768), bf),
            pltpu.VMEM((WIDE, 256), bf), pltpu.VMEM((WIDE, 256), bf),
            pltpu.VMEM((CHUNKS, 2, STEP, ROWS), f32), pltpu.VMEM((CHUNKS, 2, 2, STEP, ROWS), f32),
            pltpu.VMEM((CHUNKS, STEP, ROWS), f32), pltpu.VMEM((2, 2, LEV, 1, ROWS), f32),
            pltpu.VMEM((CHUNKS, SEGS, PART, ROWS), f32), pltpu.VMEM((CHUNKS, SEGS, PART, ROWS), f32),
            pltpu.VMEM((CHUNKS, SEGS, PART, ROWS), f32),
            pltpu.VMEM((16, 256), f32), pltpu.VMEM((SEGS, 16, 256), f32), pltpu.VMEM((2, LEV, SEGS, 256), f32),
            dma((CHUNKS, 4)), dma((3,)), dma((CHUNKS, 2)), dma((CHUNKS, 2)), dma((2, 2)), dma((2, 2)),
            dma((CHUNKS, SEGS)), dma((CHUNKS, SEGS)), dma((CHUNKS, SEGS)), dma((CHUNKS, SEGS)),
            dma((SEGS,)), dma((SEGS,)), dma((BANDS,)), dma((BANDS,)), dma((LEV + 1,)), dma((CHUNKS,)),
        ],
        compiler_params=pltpu.CompilerParams(
            collective_id=0, has_side_effects=True, vmem_limit_bytes=56 * 2**20
        ),
        cost_estimate=pl.CostEstimate(flops=10**9, bytes_accessed=16 * 10**6, transcendentals=0),
    )(
        flip(start), flip(sec), flip(zon), flip(mer), ut, pt, qt,
        cutoffs.reshape(BANDS, ROWS), rc, nest_values,
    )
    where = jnp.stack([lax.axis_index("lat"), lax.axis_index("lon")]).astype(jnp.int32)
    result = pl.pallas_call(
        finish_kernel,
        out_shape=jax.ShapeDtypeStruct((LEV, SEG, ROWS), f32),
        in_specs=[smem, smem, vmem, vmem, anywhere, anywhere],
        out_specs=anywhere,
        scratch_shapes=[
            pltpu.VMEM((LEV, 256 + 928 + 256, ROWS), f32),
            pltpu.VMEM((LEV, 128, 256), f32),
            pltpu.VMEM((RANK, 2 * ROWS), f32),
            dma((LEV,)),
            dma,
        ],
        compiler_params=pltpu.CompilerParams(vmem_limit_bytes=56 * 2**20),
        cost_estimate=pl.CostEstimate(flops=10**9, bytes_accessed=4 * 10**6, transcendentals=0),
    )(where, nest_corners, zout, eu, sect, nestg)
    return flip(result)


def solution(mesh):
    tables = make_tables()
    spec = P(None, "lat", "lon")
    return jax.shard_map(
        lambda *args: shards(*args, tables),
        mesh=mesh,
        in_specs=(spec, spec, spec, spec, P(), P(None, None, ("lat", "lon"), None), P()),
        out_specs=spec,
        check_vma=False,
    )
```

profile of v0, /device:TPU:1, one launch (start us, length us, event | category | flops | bytes accessed | tf_op | source)
XLA Modules:
  0.0 64.7 jit_solution(10307827771695545701)
XLA Ops:
  0.0 0.6 pad_add_fusion.lat_ref
  0.6 60.0 %shard_map.118 = (f32[3,8,40,128]{3,2,1,0:T(8,128)}, f32[6,900,128]{2,1,0:T(8,128)}, f32[6,128,256]{2,1,0:T(8,128)}) custom-call(f32[6,900,128]{2,1,0:T(8,128)} %bitcast.8, f32[6,900,128]{2,1,0:T(8,128)} %bitcast.9, f32[6,900,128]{2,1,0:T(8,128)} %bitcast.10, f32[6,900,128]{2,1,0:T(8,128)} %bitcast.11, bf16[320,1024]{1,0:T(8,128)(2,1)} %constant.19.clone.ut_h, ...), custom_call_target="tpu_custom_call" | custom-call | flops 1000000000 | bytes 16000000 | tf_op jit(solution)/shard_map/pallas_call | solution.py:476
  60.6 4.1 %shard_map.119 = f32[6,900,128]{2,1,0:T(8,128)} custom-call(s32[2]{0:T(128)} %pad_add_fusion.lat_ref, s32[2,2]{1,0:T(2,128)} %corners.1, f32[3,8,40,128]{3,2,1,0:T(8,128)} %get-tuple-element.8.zin, bf16[928,512]{1,0:T(8,128)(2,1)} %constant.20.clone.eu, f32[6,900,128]{2,1,0:T(8,128)} %get-tuple-element.9.sect, f32[6,128,256]{2,1,0:T(8,128)} %get-tuple-element.10.nestg), custom_call_target="tpu_custom_call" | custom-call | flops 1000000000 | bytes 4000000 | tf_op jit(solution)/shard_map/pallas_call | solution.py:507
where the time goes:
time: 64.9 us; the launch traced here: 64.7 us
  Pallas kernels  64.1 us (99%)
    pallas_call x1, Pallas kernels, shards(): pl.pallas_call(section_kernel, out_shape=(jax.ShapeDtypeStruct((CHUNKS, S...  60 us
    pallas_call x1, Pallas kernels, shards(): pl.pallas_call(finish_kernel, out_shape=jax.ShapeDtypeStruct((LEV, SEG, R...  4.07 us

commit v1 on v0

--- a/solution.py
+++ b/solution.py
@@ -16,7 +16,8 @@
 PART = RANK // 4
 CHUNKS, PAIR = 3, 2
 STEP, STEPS = 32, 29
-TALL = STEP * STEPS + 8
+CELLS = STEP * STEPS
+TALL = CELLS + 8
 WIDE = 1024
 MESH = pl.DeviceIdType.MESH
 BF = ml_dtypes.bfloat16
@@ -84,7 +85,7 @@
     uh, ul = split(basis)
     ut = np.zeros((2 * RANK, WIDE), BF)
     ut[:RANK, :SEG], ut[RANK:, :SEG] = uh.T, ul.T
-    eu = np.zeros((STEP * STEPS, 512), BF)
+    eu = np.zeros((CELLS, 512), BF)
     eu[:SEG, :RANK], eu[:SEG, RANK : 2 * RANK], eu[:SEG, 2 * RANK : 3 * RANK] = uh, uh, ul
     pt = np.zeros((4, 256, WIDE), BF)
     qt = np.zeros((4, 2 * RANK, 768), BF)
@@ -173,8 +174,8 @@
     for buf in (tb, zb, mb, sb):
         for lev in range(LEV):
             buf[lev, SEG:TALL, :] = jnp.zeros((TALL - SEG, ROWS), jnp.float32)
-    sh[STEP * STEPS :, :] = jnp.zeros((WIDE - STEP * STEPS, 256), jnp.bfloat16)
-    sl[STEP * STEPS :, :] = jnp.zeros((WIDE - STEP * STEPS, 256), jnp.bfloat16)
+    sh[CELLS :, :] = jnp.zeros((WIDE - CELLS, 256), jnp.bfloat16)
+    sl[CELLS :, :] = jnp.zeros((WIDE - CELLS, 256), jnp.bfloat16)
     pl.semaphore_wait(barrier, SEGS - 1 + BANDS - 1)
 
     left, right = lax.rem(lon + SEGS - 1, SEGS), lax.rem(lon + 1, SEGS)
@@ -215,7 +216,7 @@
             return tuple(out)
 
         none = jnp.zeros((STEP, ROWS), jnp.float32)
-        packed = lax.fori_loop(0, STEPS, pack, (none, none))
+        packed = lax.fori_loop(0, STEPS, pack, (none, none), unroll=True)
         for a in range(2):
             pk[c, a] = packed[a]
         for way, to in enumerate((after, before)):
@@ -248,6 +249,7 @@
     edge_row = rc[lat, 0:1, :]
     inverse_cos = rc[lat, 1:2, :]
     first_edge, last_edge = rc[lat, 2:3, :], rc[lat, 3:4, :]
+    tall_lane = lanes((CELLS, ROWS))
     flux_scale = jnp.where(even[:1], last_edge, first_edge)
 
     def fluxes(c, put):
@@ -266,28 +268,24 @@
             zb[lev, SEG : SEG + 1, :] = lh[1, 0, lev]
             west = 0.0625 * (lh[1, 1, lev] + zb[lev, 0:1, :]) * (lh[0, 1, lev] + tb[lev, 0:1, :])
 
-            def step(b, west, lev=lev, h=h):
-                r = pl.multiple_of(b * STEP, STEP)
-                t_all = tb[lev, pl.ds(r, STEP + 8), :]
-                z_all = zb[lev, pl.ds(r, STEP + 8), :]
-                t = t_all[:STEP]
-                east = 0.0625 * (z_all[:STEP] + z_all[1 : STEP + 1]) * (t + t_all[1 : STEP + 1])
-                zonal = east - jnp.concatenate([west, east[: STEP - 1]], axis=0)
-                m = mb[lev, pl.ds(r, STEP), :]
-                ends = pltpu.roll(fl[c], lax.rem(2 * ROWS - 1 - 4 * b - 2 * h, ROWS), 1)
-                south = edge_row * (t + pltpu.roll(t, ROWS - 1, 1)) * (m + pltpu.roll(m, ROWS - 1, 1))
-                south = jnp.where(lane == ROWS - 1, ends, south)
-                north = jnp.where(lane == 0, ends, pltpu.roll(south, 1, 1))
-                s = sb[lev, pl.ds(r, STEP), :]
-                put(lev, h, r, 0.75 * s + 0.25 * t - zonal - inverse_cos * (south - north))
-                return east[STEP - 1 : STEP]
-
-            lax.fori_loop(0, STEPS, step, west)
+            t_all, z_all = tb[lev], zb[lev]
+            t = t_all[:CELLS]
+            east = 0.0625 * (z_all[:CELLS] + z_all[1 : CELLS + 1]) * (t + t_all[1 : CELLS + 1])
+            zonal = east - jnp.concatenate([west, east[: CELLS - 1]], axis=0)
+            m = mb[lev, :CELLS, :]
+            packed = fl[c]
+            ends = jnp.concatenate(
+                [pltpu.roll(packed, (2 * ROWS - 1 - 4 * b - 2 * h) % ROWS, 1) for b in range(STEPS)], axis=0
+            )
+            south = edge_row * (t + pltpu.roll(t, ROWS - 1, 1)) * (m + pltpu.roll(m, ROWS - 1, 1))
+            south = jnp.where(tall_lane == ROWS - 1, ends, south)
+            north = jnp.where(tall_lane == 0, ends, pltpu.roll(south, 1, 1))
+            put(lev, h, 0.75 * sb[lev, :CELLS, :] + 0.25 * t - zonal - inverse_cos * (south - north))
 
     @pl.when(jnp.logical_not(polar))
     def _():
-        def put(lev, h, r, value):
-            sb[lev, pl.ds(r, STEP), :] = value
+        def put(lev, h, value):
+            sb[lev, :CELLS, :] = value
 
         outs = []
         for c in range(CHUNKS):
@@ -303,10 +301,10 @@
 
     @pl.when(polar)
     def _():
-        def put(lev, h, r, value):
+        def put(lev, h, value):
             hi, lo = hi_lo(value)
-            sh[pl.ds(r, STEP), h * ROWS : (h + 1) * ROWS] = hi
-            sl[pl.ds(r, STEP), h * ROWS : (h + 1) * ROWS] = lo
+            sh[:CELLS, h * ROWS : (h + 1) * ROWS] = hi
+            sl[:CELLS, h * ROWS : (h + 1) * ROWS] = lo
 
         block = lanes((PART, ROWS)) // 32
 
@@ -400,8 +398,8 @@
         copy.wait_send()
 
 
-def finish_kernel(lat_ref, corners, zin, eu, sect, nestg, out, ob, nb, zc, osem, nsem):
-    lat, lon = lat_ref[0], lat_ref[1]
+def finish_kernel(corners, zin, eu, sect, nestg, out, ob, nb, zc, osem, nsem):
+    lat, lon = lax.axis_index("lat"), lax.axis_index("lon")
     polar = (lat < BANDS // 4) | (lat >= BANDS - BANDS // 4)
     half = lat // (BANDS // 2)
     row = corners[half, 0] - lat * ROWS
@@ -437,7 +435,7 @@
             rhs = jnp.concatenate([hi, lo, hi, jnp.zeros((32, 2 * ROWS), jnp.bfloat16)], axis=0)
             full = dot(eu[...], rhs)
             for h in range(PAIR):
-                ob[PAIR * c + h, 256 : 256 + STEP * STEPS, :] = full[:, h * ROWS : (h + 1) * ROWS]
+                ob[PAIR * c + h, 256 : 256 + CELLS, :] = full[:, h * ROWS : (h + 1) * ROWS]
 
     @pl.when(hit)
     def _():
@@ -503,11 +501,10 @@
         flip(start), flip(sec), flip(zon), flip(mer), ut, pt, qt,
         cutoffs.reshape(BANDS, ROWS), rc, nest_values,
     )
-    where = jnp.stack([lax.axis_index("lat"), lax.axis_index("lon")]).astype(jnp.int32)
     result = pl.pallas_call(
         finish_kernel,
         out_shape=jax.ShapeDtypeStruct((LEV, SEG, ROWS), f32),
-        in_specs=[smem, smem, vmem, vmem, anywhere, anywhere],
+        in_specs=[smem, vmem, vmem, anywhere, anywhere],
         out_specs=anywhere,
         scratch_shapes=[
             pltpu.VMEM((LEV, 256 + 928 + 256, ROWS), f32),
@@ -518,7 +515,7 @@
         ],
         compiler_params=pltpu.CompilerParams(vmem_limit_bytes=56 * 2**20),
         cost_estimate=pl.CostEstimate(flops=10**9, bytes_accessed=4 * 10**6, transcendentals=0),
-    )(where, nest_corners, zout, eu, sect, nestg)
+    )(nest_corners, zout, eu, sect, nestg)
     return flip(result)
 
 

time: 64.9 us -> 38.3 us (0.59)
  Pallas kernels: 64.1 us -> 38 us
    pallas_call x1, Pallas kernels: 60 us -> 33.9 us  [shards(): pl.pallas_call(section_kernel, out_shape=(jax.ShapeDtypeStruct((CHUNKS, S...]
where the time goes in v1:
time: 38.3 us; the launch traced here: 38.1 us
  Pallas kernels  38 us (99%)
    pallas_call x1, Pallas kernels, shards(): pl.pallas_call(section_kernel, out_shape=(jax.ShapeDtypeStruct((CHUNKS, S...  33.9 us
    pallas_call x1, Pallas kernels, shards(): pl.pallas_call(finish_kernel, out_shape=jax.ShapeDtypeStruct((LEV, SEG, R...  4.07 us

profile of v1, /device:TPU:1, one launch (start us, length us, event | category | flops | bytes accessed | tf_op | source)
XLA Modules:
  0.0 38.1 jit_solution(4769595827588704035)
XLA Ops:
  0.0 33.9 %shard_map.118 = (f32[3,8,40,128]{3,2,1,0:T(8,128)}, f32[6,900,128]{2,1,0:T(8,128)}, f32[6,128,256]{2,1,0:T(8,128)}) custom-call(f32[6,900,128]{2,1,0:T(8,128)} %bitcast.6, f32[6,900,128]{2,1,0:T(8,128)} %bitcast.7, f32[6,900,128]{2,1,0:T(8,128)} %bitcast.8, f32[6,900,128]{2,1,0:T(8,128)} %bitcast.9, bf16[320,1024]{1,0:T(8,128)(2,1)} %constant.10.clone.ut_h, ...), custom_call_target="tpu_custom_call" | custom-call | flops 1000000000 | bytes 16000000 | tf_op jit(solution)/shard_map/pallas_call | solution.py:474
  33.9 4.1 %shard_map.119 = f32[6,900,128]{2,1,0:T(8,128)} custom-call(s32[2,2]{1,0:T(2,128)} %corners.1, f32[3,8,40,128]{3,2,1,0:T(8,128)} %get-tuple-element.8.zin, bf16[928,512]{1,0:T(8,128)(2,1)} %constant.11.clone.eu, f32[6,900,128]{2,1,0:T(8,128)} %get-tuple-element.9.sect, f32[6,128,256]{2,1,0:T(8,128)} %get-tuple-element.10.nestg), custom_call_target="tpu_custom_call" | custom-call | flops 1000000000 | bytes 4000000 | tf_op jit(solution)/shard_map/pallas_call | solution.py:504

commit v2 on v1

--- a/solution.py
+++ b/solution.py
@@ -1,3 +1,4 @@
+import functools
 import math
 
 import jax
@@ -119,8 +120,9 @@
     rc = np.zeros((BANDS, 8, ROWS), np.float32)
     for b in range(BANDS):
         r0 = b * ROWS
-        rc[b, 0] = 0.0625 * edge[r0 + 1 : r0 + ROWS + 1]
+        rc[b, 0, : ROWS - 1] = 0.0625 * edge[r0 + 1 : r0 + ROWS]
         rc[b, 1] = (1.0 / center[r0 : r0 + ROWS]).astype(np.float32)
+        rc[b, 4, 0], rc[b, 4, ROWS - 1] = rc[b, 1, 0], -rc[b, 1, ROWS - 1]
         rc[b, 2] = 0.0625 * edge[r0]
         rc[b, 3] = 0.0625 * edge[r0 + ROWS]
     return ut, eu, pt, qt, rc
@@ -142,53 +144,94 @@
 def section_kernel(
     start, sec, zon, mer, ut_h, pt_h, qt_h, cut, rc, nest,
     zout, sect, nestg,
-    sb, tb, zb, mb, ut, pt, qt, sh, sl, pk, pkr, fl, lh,
+    sb, tb, zb, mb, ut, pt, qt, sh, sl, pk, pkr, lh,
     fsend, recv, bsend, nsend, ngat, nasm,
     ld, tabs, psend, precv, lsend, lrecv, fs, fr, bs, br, n1s, n1r, n2s, n2r, osem, zsem,
 ):
     lat, lon = lax.axis_index("lat"), lax.axis_index("lon")
     polar = (lat < BANDS // 4) | (lat >= BANDS - BANDS // 4)
-
-    loads = []
-    for c in range(CHUNKS):
-        pair = pl.ds(PAIR * c, PAIR)
-        loads.append([])
-        for a, (src, dst) in enumerate(((sec, tb), (mer, mb), (zon, zb), (start, sb))):
-            copy = pltpu.make_async_copy(src.at[pair], dst.at[pair, pl.ds(0, SEG)], ld.at[c, a])
-            copy.start()
-            loads[c].append(copy)
+    core = lax.rem(lon, 2)
+
+    barrier = pltpu.get_barrier_semaphore()
+    for k in range(1, SEGS):
+        pl.semaphore_signal(barrier, inc=1, device_id=(lat, lax.rem(lon + k, SEGS)), device_id_type=MESH)
+    for k in range(1, BANDS):
+        pl.semaphore_signal(barrier, inc=1, device_id=(lax.rem(lat + k, BANDS), lon), device_id_type=MESH)
+
+    loads = [[None] * 4 for _ in range(CHUNKS)]
+    for late in range(2):
+        for c in range(CHUNKS):
+            pair = pl.ds(PAIR * c, PAIR)
+            for a, (src, dst) in enumerate(((sec, tb), (mer, mb)) if late == 0 else ((zon, zb), (start, sb))):
+                copy = pltpu.make_async_copy(src.at[pair], dst.at[pair, pl.ds(0, SEG)], ld.at[c, 2 * late + a])
+                copy.start()
+                loads[c][2 * late + a] = copy
     tables = [
         pltpu.make_async_copy(src, dst, tabs.at[n]) for n, (src, dst) in enumerate(((ut_h, ut), (pt_h, pt), (qt_h, qt)))
     ]
     for copy in tables:
         copy.start()
 
-    barrier = pltpu.get_barrier_semaphore()
-    for k in range(1, SEGS):
-        pl.semaphore_signal(barrier, inc=1, device_id=(lat, lax.rem(lon + k, SEGS)), device_id_type=MESH)
-    for k in range(1, BANDS):
-        pl.semaphore_signal(barrier, inc=1, device_id=(lax.rem(lat + k, BANDS), lon), device_id_type=MESH)
     for n in range(12):
         nsend[n : n + 1, :] = nest[n // 6, n % 6]
     nsend[12:16, :] = jnp.zeros((4, 256), jnp.float32)
     for buf in (tb, zb, mb, sb):
         for lev in range(LEV):
             buf[lev, SEG:TALL, :] = jnp.zeros((TALL - SEG, ROWS), jnp.float32)
-    sh[CELLS :, :] = jnp.zeros((WIDE - CELLS, 256), jnp.bfloat16)
-    sl[CELLS :, :] = jnp.zeros((WIDE - CELLS, 256), jnp.bfloat16)
-    pl.semaphore_wait(barrier, SEGS - 1 + BANDS - 1)
-
+    for c in range(CHUNKS):
+        sh[c, CELLS:, :] = jnp.zeros((WIDE - CELLS, 256), jnp.bfloat16)
+        sl[c, CELLS:, :] = jnp.zeros((WIDE - CELLS, 256), jnp.bfloat16)
+
+    lane = lanes((STEP, ROWS))
+    even = (lane & 1) == 0
+    before, after = lax.rem(lat + BANDS - 1, BANDS), lax.rem(lat + 1, BANDS)
     left, right = lax.rem(lon + SEGS - 1, SEGS), lax.rem(lon + 1, SEGS)
-    lon_copies = []
-    for a, src in enumerate((sec, zon)):
-        for way, (row, to) in enumerate(((0, left), (SEG - 1, right))):
+    has_before, has_after = lat > 0, lat < BANDS - 1
+    lat_copies, lon_copies, nest_copies = [], [], []
+    for c in range(CHUNKS):
+        loads[c][0].wait()
+        loads[c][1].wait()
+
+        def pack(b, acc, c=c):
+            out = []
+            for buf, x in zip((tb, mb), acc):
+                for h in range(PAIR):
+                    v = buf[PAIR * c + h, pl.ds(pl.multiple_of(b * STEP, STEP), STEP), :]
+                    x = jnp.where((lane >> 1) == 2 * b + h, pltpu.roll(v, lax.rem(4 * b + 2 * h + 1, ROWS), 1), x)
+                out.append(x)
+            return tuple(out)
+
+        none = jnp.zeros((STEP, ROWS), jnp.float32)
+        packed = lax.fori_loop(0, STEPS, pack, (none, none), unroll=True)
+        for a in range(2):
+            pk[c, a] = packed[a]
+        if c == 0:
+            pl.semaphore_wait(barrier, SEGS - 1 + BANDS - 1)
+        for way, (to, there_is) in enumerate(((after, has_after), (before, has_before))):
             copy = pltpu.make_async_remote_copy(
-                src_ref=src.at[:, pl.ds(row, 1), :], dst_ref=lh.at[a, way], send_sem=lsend.at[a, way],
-                recv_sem=lrecv.at[a, way], device_id=(lat, to), device_id_type=MESH,
+                src_ref=pk.at[c], dst_ref=pkr.at[c, way], send_sem=psend.at[c, way], recv_sem=precv.at[c, way],
+                device_id=(to, lon), device_id_type=MESH,
             )
-            copy.start()
-            lon_copies.append(copy)
-    nest_copies = []
+            pl.when(there_is)(copy.start)
+            lat_copies.append(copy)
+        if c == 0:
+            for a, src in enumerate((sec, zon)):
+                for way, (row, to) in enumerate(((0, left), (SEG - 1, right))):
+                    copy = pltpu.make_async_remote_copy(
+                        src_ref=src.at[:, pl.ds(row, 1), :], dst_ref=lh.at[a, way], send_sem=lsend.at[a, way],
+                        recv_sem=lrecv.at[a, way], device_id=(lat, to), device_id_type=MESH,
+                    )
+                    copy.start()
+                    lon_copies.append(copy)
+
+    for way, there_is in enumerate((has_before, has_after)):
+
+        @pl.when(jnp.logical_not(there_is))
+        def _(way=way):
+            for c in range(CHUNKS):
+                for a in range(2):
+                    pkr[c, way, a] = jnp.zeros((STEP, ROWS), jnp.float32)
+
     for k in range(1, SEGS):
         copy = pltpu.make_async_remote_copy(
             src_ref=nsend, dst_ref=ngat.at[lon], send_sem=n1s.at[k], recv_sem=n1r.at[k],
@@ -198,89 +241,82 @@
         nest_copies.append(copy)
     ngat[lon] = nsend[...]
 
-    before, after = lax.rem(lat + BANDS - 1, BANDS), lax.rem(lat + 1, BANDS)
-    lane = lanes((STEP, ROWS))
-    even = (lane & 1) == 0
-    lat_copies = []
+    edge_row = rc[lat, 0:1, :]
+    inverse_cos = rc[lat, 1:2, :]
+    first_edge, last_edge = rc[lat, 2:3, :], rc[lat, 3:4, :]
+    end_scale = rc[lat, 4:5, :]
+    flux_scale = jnp.where(even[:1], last_edge, first_edge)
+
+    def inner(c):
+        for copy in loads[c][2:]:
+            copy.wait()
+        for lev in range(PAIR * c, PAIR * c + PAIR):
+            t_all, z_all = tb[lev], zb[lev]
+            t = t_all[:CELLS]
+            east = 0.0625 * (z_all[:CELLS] + z_all[1 : CELLS + 1]) * (t + t_all[1 : CELLS + 1])
+            zonal = east - jnp.concatenate([jnp.zeros((1, ROWS), jnp.float32), east[: CELLS - 1]], axis=0)
+            m = mb[lev, :CELLS, :]
+            south = edge_row * (t + pltpu.roll(t, ROWS - 1, 1)) * (m + pltpu.roll(m, ROWS - 1, 1))
+            north = pltpu.roll(south, 1, 1)
+            sb[lev, :CELLS, :] = 0.75 * sb[lev, :CELLS, :] + 0.25 * t - zonal - inverse_cos * (south - north)
+
     for c in range(CHUNKS):
-        loads[c][0].wait()
-        loads[c][1].wait()
-
-        def pack(b, acc, c=c):
-            out = []
-            for buf, x in zip((tb, mb), acc):
-                for h in range(PAIR):
-                    v = buf[PAIR * c + h, pl.ds(pl.multiple_of(b * STEP, STEP), STEP), :]
-                    x = jnp.where((lane >> 1) == 2 * b + h, pltpu.roll(v, lax.rem(4 * b + 2 * h + 1, ROWS), 1), x)
-                out.append(x)
-            return tuple(out)
-
-        none = jnp.zeros((STEP, ROWS), jnp.float32)
-        packed = lax.fori_loop(0, STEPS, pack, (none, none), unroll=True)
-        for a in range(2):
-            pk[c, a] = packed[a]
-        for way, to in enumerate((after, before)):
-            copy = pltpu.make_async_remote_copy(
-                src_ref=pk.at[c], dst_ref=pkr.at[c, way], send_sem=psend.at[c, way], recv_sem=precv.at[c, way],
-                device_id=(to, lon), device_id_type=MESH,
-            )
-            copy.start()
-            lat_copies.append(copy)
-
-    for copy in nest_copies:
-        copy.wait_recv()
-    for n in range(12):
-        nasm[n // 6, n % 6] = jnp.concatenate([ngat[d, n : n + 1, :] for d in range(SEGS)], axis=0)
+        inner(c)
+
+    eight = pl.ds(pl.multiple_of(lat * SEGS, SEGS), SEGS)
+    mine, other = pl.ds(LEV // 2 * core, LEV // 2), pl.ds(LEV // 2 * (1 - core), LEV // 2)
     spread = []
-    eight = pl.ds(pl.multiple_of(lat * SEGS, SEGS), SEGS)
     for k in range(1, BANDS):
         to = lax.rem(lat + k, BANDS)
         copy = pltpu.make_async_remote_copy(
-            src_ref=nasm.at[to // (BANDS // 2)], dst_ref=nestg.at[:, eight, :], send_sem=n2s.at[k],
+            src_ref=nasm.at[to // (BANDS // 2), mine], dst_ref=nestg.at[mine, eight, :], send_sem=n2s.at[k],
             recv_sem=n2r.at[k], device_id=(to, lon), device_id_type=MESH,
         )
-        copy.start()
         spread.append(copy)
-    own_nest = pltpu.make_async_copy(nasm.at[lat // (BANDS // 2)], nestg.at[:, eight, :], osem.at[LEV])
-    own_nest.start()
+    own_nest = pltpu.make_async_copy(nasm.at[lat // (BANDS // 2), mine], nestg.at[mine, eight, :], osem.at[LEV])
+    swap = pltpu.make_async_remote_copy(
+        src_ref=nestg.at[mine], dst_ref=nestg.at[mine], send_sem=n2s.at[0], recv_sem=n2r.at[0],
+        device_id=(lat, lon + 1 - 2 * core), device_id_type=MESH,
+    )
+
+    def spread_nest():
+        for copy in nest_copies:
+            copy.wait_recv()
+        for n in range(12):
+            nasm[n // 6, n % 6] = jnp.concatenate([ngat[d, n : n + 1, :] for d in range(SEGS)], axis=0)
+        for copy in spread:
+            copy.start()
+        own_nest.start()
+
+    def swap_nest():
+        for copy in spread:
+            copy.wait_recv()
+        own_nest.wait()
+        swap.start()
 
     for copy in lon_copies:
         copy.wait_recv()
-    edge_row = rc[lat, 0:1, :]
-    inverse_cos = rc[lat, 1:2, :]
-    first_edge, last_edge = rc[lat, 2:3, :], rc[lat, 3:4, :]
-    tall_lane = lanes((CELLS, ROWS))
-    flux_scale = jnp.where(even[:1], last_edge, first_edge)
-
-    def fluxes(c, put):
-        for copy in loads[c][2:]:
-            copy.wait()
-        for way in range(2):
-            lat_copies[2 * c + way].wait_recv()
+
+    def borders(c, put):
+        for way, there_is in enumerate((has_before, has_after)):
+            pl.when(there_is)(lat_copies[2 * c + way].wait_recv)
         sums = [
             pk[c, a] + jnp.where(even, pltpu.roll(pkr[c, 1, a], ROWS - 1, 1), pltpu.roll(pkr[c, 0, a], 1, 1))
             for a in range(2)
         ]
-        fl[c] = sums[0] * sums[1] * flux_scale
+        packed = sums[0] * sums[1] * flux_scale
         for h in range(PAIR):
             lev = PAIR * c + h
-            tb[lev, SEG : SEG + 1, :] = lh[0, 0, lev]
-            zb[lev, SEG : SEG + 1, :] = lh[1, 0, lev]
-            west = 0.0625 * (lh[1, 1, lev] + zb[lev, 0:1, :]) * (lh[0, 1, lev] + tb[lev, 0:1, :])
-
-            t_all, z_all = tb[lev], zb[lev]
-            t = t_all[:CELLS]
-            east = 0.0625 * (z_all[:CELLS] + z_all[1 : CELLS + 1]) * (t + t_all[1 : CELLS + 1])
-            zonal = east - jnp.concatenate([west, east[: CELLS - 1]], axis=0)
-            m = mb[lev, :CELLS, :]
-            packed = fl[c]
+            t0, z0 = tb[lev, 0:1, :], zb[lev, 0:1, :]
+            t1, z1 = tb[lev, SEG - 1 : SEG, :], zb[lev, SEG - 1 : SEG, :]
+            west = 0.0625 * (lh[1, 1, lev] + z0) * (lh[0, 1, lev] + t0)
+            east = 0.0625 * (lh[1, 0, lev] + z1) * (lh[0, 0, lev] + t1)
+            sb[lev, 0:1, :] = sb[lev, 0:1, :] + west
+            sb[lev, SEG - 1 : SEG, :] = sb[lev, SEG - 1 : SEG, :] - (east - 0.0625 * z1 * t1)
             ends = jnp.concatenate(
                 [pltpu.roll(packed, (2 * ROWS - 1 - 4 * b - 2 * h) % ROWS, 1) for b in range(STEPS)], axis=0
             )
-            south = edge_row * (t + pltpu.roll(t, ROWS - 1, 1)) * (m + pltpu.roll(m, ROWS - 1, 1))
-            south = jnp.where(tall_lane == ROWS - 1, ends, south)
-            north = jnp.where(tall_lane == 0, ends, pltpu.roll(south, 1, 1))
-            put(lev, h, 0.75 * sb[lev, :CELLS, :] + 0.25 * t - zonal - inverse_cos * (south - north))
+            put(lev, h, sb[lev, :CELLS, :] + end_scale * ends)
 
     @pl.when(jnp.logical_not(polar))
     def _():
@@ -289,11 +325,14 @@
 
         outs = []
         for c in range(CHUNKS):
-            fluxes(c, put)
+            borders(c, put)
+            if c == 0:
+                spread_nest()
             pair = pl.ds(PAIR * c, PAIR)
             copy = pltpu.make_async_copy(sb.at[pair, pl.ds(0, SEG)], sect.at[pair], osem.at[c])
             copy.start()
             outs.append(copy)
+        swap_nest()
         for copy in outs:
             copy.wait()
         for copy in tables:
@@ -301,10 +340,10 @@
 
     @pl.when(polar)
     def _():
-        def put(lev, h, value):
+        def put(c, lev, h, value):
             hi, lo = hi_lo(value)
-            sh[:CELLS, h * ROWS : (h + 1) * ROWS] = hi
-            sl[:CELLS, h * ROWS : (h + 1) * ROWS] = lo
+            sh[c, :CELLS, h * ROWS : (h + 1) * ROWS] = hi
+            sl[c, :CELLS, h * ROWS : (h + 1) * ROWS] = lo
 
         block = lanes((PART, ROWS)) // 32
 
@@ -316,11 +355,11 @@
 
         there = []
         for c in range(CHUNKS):
-            fluxes(c, put)
+            borders(c, functools.partial(put, c))
             if c == 0:
                 tables[0].wait()
-            both = dot(ut[...], sh[...])
-            y = both[:RANK] + both[RANK:] + dot(ut[:RANK, :], sl[...])
+            both = dot(ut[...], sh[c])
+            y = both[:RANK] + both[RANK:] + dot(ut[:RANK, :], sl[c])
             for h in range(PAIR):
                 for q in range(4):
                     acc = None
@@ -334,6 +373,8 @@
             there.append([exchange(c, k, fsend, recv, fs, fr) for k in range(1, SEGS)])
             for copy in there[c]:
                 copy.start()
+            if c == 0:
+                spread_nest()
 
         tables[1].wait()
         tables[2].wait()
@@ -383,6 +424,7 @@
             copy = pltpu.make_async_copy(bsend.at[c, lon], zout.at[c, lon], zsem.at[c])
             copy.start()
             own.append(copy)
+        swap_nest()
         for c in range(CHUNKS):
             own[c].wait()
             for copy in back[c]:
@@ -391,21 +433,40 @@
             for copy in there[c] + back[c]:
                 copy.wait_send()
 
-    for copy in spread:
-        copy.wait_recv()
-    own_nest.wait()
-    for copy in lon_copies + nest_copies + lat_copies + spread:
+    swap.wait()
+    for copy in lon_copies + nest_copies + spread:
         copy.wait_send()
-
-
-def finish_kernel(corners, zin, eu, sect, nestg, out, ob, nb, zc, osem, nsem):
+    for n, copy in enumerate(lat_copies):
+        pl.when((has_after, has_before)[n % 2])(copy.wait_send)
+
+
+def finish_kernel(corners, zin, eu, sect, nestg, out, ob, nb, zc, osem, ssem, nsem):
     lat, lon = lax.axis_index("lat"), lax.axis_index("lon")
     polar = (lat < BANDS // 4) | (lat >= BANDS - BANDS // 4)
     half = lat // (BANDS // 2)
     row = corners[half, 0] - lat * ROWS
     col = corners[half, 1] - lon * SEG
     hit = (row > -ROWS) & (row < ROWS) & (col > -256) & (col < SEG)
+    miss = jnp.logical_not(hit)
     fetch = pltpu.make_async_copy(nestg, nb, nsem)
+    copies = [
+        pltpu.make_async_copy(
+            ob.at[pl.ds(PAIR * c, PAIR), pl.ds(256, SEG), :], out.at[pl.ds(PAIR * c, PAIR)], osem.at[c]
+        )
+        for c in range(CHUNKS)
+    ]
+    fills = [
+        pltpu.make_async_copy(
+            sect.at[pl.ds(PAIR * c, PAIR)], ob.at[pl.ds(PAIR * c, PAIR), pl.ds(256, SEG), :], ssem.at[c]
+        )
+        for c in range(CHUNKS)
+    ]
+    block = lanes((PART, ROWS)) // 32
+
+    @pl.when(jnp.logical_not(polar))
+    def _():
+        for copy in fills:
+            copy.start()
 
     @pl.when(hit)
     def _():
@@ -413,11 +474,12 @@
 
     @pl.when(jnp.logical_not(polar))
     def _():
-        copy = pltpu.make_async_copy(sect, ob.at[:, pl.ds(256, SEG), :], osem.at[0])
-        copy.start()
-        copy.wait()
-
-    block = lanes((PART, ROWS)) // 32
+        for c in range(CHUNKS):
+            fills[c].wait()
+
+            @pl.when(miss)
+            def _():
+                copies[c].start()
 
     @pl.when(polar)
     def _():
@@ -437,6 +499,10 @@
             for h in range(PAIR):
                 ob[PAIR * c + h, 256 : 256 + CELLS, :] = full[:, h * ROWS : (h + 1) * ROWS]
 
+            @pl.when(miss)
+            def _():
+                copies[c].start()
+
     @pl.when(hit)
     def _():
         fetch.wait()
@@ -452,12 +518,9 @@
             tall = pltpu.roll(pltpu.roll(tall, off, 0), lax.rem(row + ROWS, ROWS), 1)
             here = ob[lev, pl.ds(base, 264), :]
             ob[lev, pl.ds(base, 264), :] = jnp.where(inside, tall, here)
-
-    copies = []
-    for lev in range(LEV):
-        copy = pltpu.make_async_copy(ob.at[lev, pl.ds(256, SEG), :], out.at[lev], osem.at[lev])
-        copy.start()
-        copies.append(copy)
+            if lev % PAIR == PAIR - 1:
+                copies[lev // PAIR].start()
+
     for copy in copies:
         copy.wait()
 
@@ -483,9 +546,9 @@
         scratch_shapes=[
             field, field, field, field,
             pltpu.VMEM((2 * RANK, WIDE), bf), pltpu.VMEM((4, 256, WIDE), bf), pltpu.VMEM((4, 2 * RANK, 768), bf),
-            pltpu.VMEM((WIDE, 256), bf), pltpu.VMEM((WIDE, 256), bf),
+            pltpu.VMEM((CHUNKS, WIDE, 256), bf), pltpu.VMEM((CHUNKS, WIDE, 256), bf),
             pltpu.VMEM((CHUNKS, 2, STEP, ROWS), f32), pltpu.VMEM((CHUNKS, 2, 2, STEP, ROWS), f32),
-            pltpu.VMEM((CHUNKS, STEP, ROWS), f32), pltpu.VMEM((2, 2, LEV, 1, ROWS), f32),
+            pltpu.VMEM((2, 2, LEV, 1, ROWS), f32),
             pltpu.VMEM((CHUNKS, SEGS, PART, ROWS), f32), pltpu.VMEM((CHUNKS, SEGS, PART, ROWS), f32),
             pltpu.VMEM((CHUNKS, SEGS, PART, ROWS), f32),
             pltpu.VMEM((16, 256), f32), pltpu.VMEM((SEGS, 16, 256), f32), pltpu.VMEM((2, LEV, SEGS, 256), f32),
@@ -510,7 +573,8 @@
             pltpu.VMEM((LEV, 256 + 928 + 256, ROWS), f32),
             pltpu.VMEM((LEV, 128, 256), f32),
             pltpu.VMEM((RANK, 2 * ROWS), f32),
-            dma((LEV,)),
+            dma((CHUNKS,)),
+            dma((CHUNKS,)),
             dma,
         ],
         compiler_params=pltpu.CompilerParams(vmem_limit_bytes=56 * 2**20),

time: 38.3 us -> 36.9 us (0.963)
  Pallas kernels: 38 us -> 36.5 us
    pallas_call x1, Pallas kernels: 33.9 us -> 32.8 us  [shards(): pl.pallas_call(section_kernel, out_shape=(jax.ShapeDtypeStruct((CHUNKS, S...]
where the time goes in v2:
time: 36.9 us; the launch traced here: 36.7 us
  Pallas kernels  36.5 us (99%)
    pallas_call x1, Pallas kernels, shards(): pl.pallas_call(section_kernel, out_shape=(jax.ShapeDtypeStruct((CHUNKS, S...  32.8 us
    pallas_call x1, Pallas kernels, shards(): pl.pallas_call(finish_kernel, out_shape=jax.ShapeDtypeStruct((LEV, SEG, R...  3.76 us

profile of v2, /device:TPU:1, one launch (start us, length us, event | category | flops | bytes accessed | tf_op | source)
XLA Modules:
  0.0 36.7 jit_solution(11173324112101110596)
XLA Ops:
  0.0 32.8 %shard_map.118 = (f32[3,8,40,128]{3,2,1,0:T(8,128)}, f32[6,900,128]{2,1,0:T(8,128)}, f32[6,128,256]{2,1,0:T(8,128)}) custom-call(f32[6,900,128]{2,1,0:T(8,128)} %bitcast.6, f32[6,900,128]{2,1,0:T(8,128)} %bitcast.7, f32[6,900,128]{2,1,0:T(8,128)} %bitcast.8, f32[6,900,128]{2,1,0:T(8,128)} %bitcast.9, bf16[320,1024]{1,0:T(8,128)(2,1)} %constant.10.clone.ut_h, ...), custom_call_target="tpu_custom_call" | custom-call | flops 1000000000 | bytes 16000000 | tf_op jit(solution)/shard_map/pallas_call | solution.py:537
  32.8 3.8 %shard_map.119 = f32[6,900,128]{2,1,0:T(8,128)} custom-call(s32[2,2]{1,0:T(2,128)} %corners.1, f32[3,8,40,128]{3,2,1,0:T(8,128)} %get-tuple-element.8.zin, bf16[928,512]{1,0:T(8,128)(2,1)} %constant.11.clone.eu, f32[6,900,128]{2,1,0:T(8,128)} %get-tuple-element.9.sect, f32[6,128,256]{2,1,0:T(8,128)} %get-tuple-element.10.nestg), custom_call_target="tpu_custom_call" | custom-call | flops 1000000000 | bytes 4000000 | tf_op jit(solution)/shard_map/pallas_call | solution.py:567

commit v3 on v2

--- a/solution.py
+++ b/solution.py
@@ -88,8 +88,8 @@
     ut[:RANK, :SEG], ut[RANK:, :SEG] = uh.T, ul.T
     eu = np.zeros((CELLS, 512), BF)
     eu[:SEG, :RANK], eu[:SEG, RANK : 2 * RANK], eu[:SEG, 2 * RANK : 3 * RANK] = uh, uh, ul
-    pt = np.zeros((4, 256, WIDE), BF)
-    qt = np.zeros((4, 2 * RANK, 768), BF)
+    pt = np.zeros((4, 256, 4 * RANK), BF)
+    qt = np.zeros((4, 2 * RANK, 512), BF)
     for g in range(4):
         s1, s2 = g, (4 if g == 0 else 8 - g)
         k1, k2 = np.arange(64) * 8 + s1, np.arange(64) * 8 + s2
@@ -108,9 +108,9 @@
                 ]
             )
         ph, pl_ = split(p.T)
-        pt[g, :, :320], pt[g, :, 320:640], pt[g, :, 640:960] = ph, ph, pl_
+        pt[g, :, : 2 * RANK], pt[g, :, 2 * RANK :] = ph, pl_
         qh, ql = split(q)
-        qt[g, :, :256], qt[g, :, 256:512], qt[g, :, 512:] = qh, qh, ql
+        qt[g, :, :256], qt[g, :, 256:] = qh, ql
     step = np.float32(math.pi / NLAT)
     half = np.float32(math.pi / 2)
     e = np.arange(NLAT + 1)
@@ -141,6 +141,15 @@
     return jnp.dot(a, b, preferred_element_type=jnp.float32)
 
 
+def split_dot(table, x):
+    hi, lo = hi_lo(x)
+    rhs = jnp.concatenate(
+        [jnp.concatenate([hi, lo], axis=1), jnp.concatenate([hi, jnp.zeros_like(lo)], axis=1)], axis=0
+    )
+    both = dot(table, rhs)
+    return both[:, : x.shape[1]] + both[:, x.shape[1] :]
+
+
 def section_kernel(
     start, sec, zon, mer, ut_h, pt_h, qt_h, cut, rc, nest,
     zout, sect, nestg,
@@ -158,18 +167,19 @@
     for k in range(1, BANDS):
         pl.semaphore_signal(barrier, inc=1, device_id=(lax.rem(lat + k, BANDS), lon), device_id_type=MESH)
 
-    loads = [[None] * 4 for _ in range(CHUNKS)]
-    for late in range(2):
-        for c in range(CHUNKS):
-            pair = pl.ds(PAIR * c, PAIR)
-            for a, (src, dst) in enumerate(((sec, tb), (mer, mb)) if late == 0 else ((zon, zb), (start, sb))):
-                copy = pltpu.make_async_copy(src.at[pair], dst.at[pair, pl.ds(0, SEG)], ld.at[c, 2 * late + a])
-                copy.start()
-                loads[c][2 * late + a] = copy
+    loads = [
+        [
+            pltpu.make_async_copy(
+                src.at[pl.ds(PAIR * c, PAIR)], dst.at[pl.ds(PAIR * c, PAIR), pl.ds(0, SEG)], ld.at[c, a]
+            )
+            for a, (src, dst) in enumerate(((sec, tb), (mer, mb), (zon, zb), (start, sb)))
+        ]
+        for c in range(CHUNKS)
+    ]
     tables = [
         pltpu.make_async_copy(src, dst, tabs.at[n]) for n, (src, dst) in enumerate(((ut_h, ut), (pt_h, pt), (qt_h, qt)))
     ]
-    for copy in tables:
+    for copy in loads[0] + tables[:1] + loads[1] + loads[2] + tables[1:]:
         copy.start()
 
     for n in range(12):
@@ -188,7 +198,7 @@
     left, right = lax.rem(lon + SEGS - 1, SEGS), lax.rem(lon + 1, SEGS)
     has_before, has_after = lat > 0, lat < BANDS - 1
     lat_copies, lon_copies, nest_copies = [], [], []
-    for c in range(CHUNKS):
+    def send_halo(c):
         loads[c][0].wait()
         loads[c][1].wait()
 
@@ -224,6 +234,7 @@
                     copy.start()
                     lon_copies.append(copy)
 
+    send_halo(0)
     for way, there_is in enumerate((has_before, has_after)):
 
         @pl.when(jnp.logical_not(there_is))
@@ -260,8 +271,9 @@
             north = pltpu.roll(south, 1, 1)
             sb[lev, :CELLS, :] = 0.75 * sb[lev, :CELLS, :] + 0.25 * t - zonal - inverse_cos * (south - north)
 
-    for c in range(CHUNKS):
-        inner(c)
+    inner(0)
+    for c in range(1, CHUNKS):
+        send_halo(c)
 
     eight = pl.ds(pl.multiple_of(lat * SEGS, SEGS), SEGS)
     mine, other = pl.ds(LEV // 2 * core, LEV // 2), pl.ds(LEV // 2 * (1 - core), LEV // 2)
@@ -294,10 +306,10 @@
         own_nest.wait()
         swap.start()
 
-    for copy in lon_copies:
-        copy.wait_recv()
-
     def borders(c, put):
+        if c == 0:
+            for copy in lon_copies:
+                copy.wait_recv()
         for way, there_is in enumerate((has_before, has_after)):
             pl.when(there_is)(lat_copies[2 * c + way].wait_recv)
         sums = [
@@ -325,6 +337,8 @@
 
         outs = []
         for c in range(CHUNKS):
+            if c:
+                inner(c)
             borders(c, put)
             if c == 0:
                 spread_nest()
@@ -355,6 +369,8 @@
 
         there = []
         for c in range(CHUNKS):
+            if c:
+                inner(c)
             borders(c, functools.partial(put, c))
             if c == 0:
                 tables[0].wait()
@@ -395,13 +411,10 @@
                 tall = jnp.concatenate(
                     [x if j == 0 else pltpu.roll(x, ROWS - 32 * j, 1) for x in two for j in range(4)], axis=0
                 )
-                hi, lo = hi_lo(tall)
-                rhs = jnp.concatenate([hi, lo, hi, jnp.zeros((WIDE - 960, ROWS), jnp.bfloat16)], axis=0)
-                wave = dot(pt[g], rhs)
+                wave = split_dot(pt[g], tall)
                 number = 8 * (n & 63) + jnp.where((n & 64) == 0, g, 4 if g == 0 else 8 - g)
                 wave = jnp.where(number <= rows_cut, wave, 0.0)
-                hi, lo = hi_lo(wave)
-                full = dot(qt[g], jnp.concatenate([hi, lo, hi], axis=0))
+                full = split_dot(qt[g], wave)
                 for x in range(2):
                     acc = None
                     for j in range(4):
@@ -545,7 +558,7 @@
         out_specs=(anywhere,) * 3,
         scratch_shapes=[
             field, field, field, field,
-            pltpu.VMEM((2 * RANK, WIDE), bf), pltpu.VMEM((4, 256, WIDE), bf), pltpu.VMEM((4, 2 * RANK, 768), bf),
+            pltpu.VMEM((2 * RANK, WIDE), bf), pltpu.VMEM((4, 256, 4 * RANK), bf), pltpu.VMEM((4, 2 * RANK, 512), bf),
             pltpu.VMEM((CHUNKS, WIDE, 256), bf), pltpu.VMEM((CHUNKS, WIDE, 256), bf),
             pltpu.VMEM((CHUNKS, 2, STEP, ROWS), f32), pltpu.VMEM((CHUNKS, 2, 2, STEP, ROWS), f32),
             pltpu.VMEM((2, 2, LEV, 1, ROWS), f32),

time: 36.9 us -> 34.1 us (0.924)
  Pallas kernels: 36.5 us -> 33.8 us
    pallas_call x1, Pallas kernels: 32.8 us -> 30 us  [shards(): pl.pallas_call(section_kernel, out_shape=(jax.ShapeDtypeStruct((CHUNKS, S...]
where the time goes in v3:
time: 34.1 us; the launch traced here: 34 us
  Pallas kernels  33.8 us (99%)
    pallas_call x1, Pallas kernels, shards(): pl.pallas_call(section_kernel, out_shape=(jax.ShapeDtypeStruct((CHUNKS, S...  30 us
    pallas_call x1, Pallas kernels, shards(): pl.pallas_call(finish_kernel, out_shape=jax.ShapeDtypeStruct((LEV, SEG, R...  3.76 us

profile of v3, /device:TPU:1, one launch (start us, length us, event | category | flops | bytes accessed | tf_op | source)
XLA Modules:
  0.0 34.0 jit_solution(11190723757841053942)
XLA Ops:
  0.0 30.0 %shard_map.118 = (f32[3,8,40,128]{3,2,1,0:T(8,128)}, f32[6,900,128]{2,1,0:T(8,128)}, f32[6,128,256]{2,1,0:T(8,128)}) custom-call(f32[6,900,128]{2,1,0:T(8,128)} %bitcast.6, f32[6,900,128]{2,1,0:T(8,128)} %bitcast.7, f32[6,900,128]{2,1,0:T(8,128)} %bitcast.8, f32[6,900,128]{2,1,0:T(8,128)} %bitcast.9, bf16[320,1024]{1,0:T(8,128)(2,1)} %constant.10.clone.ut_h, ...), custom_call_target="tpu_custom_call" | custom-call | flops 1000000000 | bytes 16000000 | tf_op jit(solution)/shard_map/pallas_call | solution.py:550
  30.0 3.8 %shard_map.119 = f32[6,900,128]{2,1,0:T(8,128)} custom-call(s32[2,2]{1,0:T(2,128)} %corners.1, f32[3,8,40,128]{3,2,1,0:T(8,128)} %get-tuple-element.8.zin, bf16[928,512]{1,0:T(8,128)(2,1)} %constant.11.clone.eu, f32[6,900,128]{2,1,0:T(8,128)} %get-tuple-element.9.sect, f32[6,128,256]{2,1,0:T(8,128)} %get-tuple-element.10.nestg), custom_call_target="tpu_custom_call" | custom-call | flops 1000000000 | bytes 4000000 | tf_op jit(solution)/shard_map/pallas_call | solution.py:580

commit v4 on v3

--- a/solution.py
+++ b/solution.py
@@ -20,6 +20,7 @@
 CELLS = STEP * STEPS
 TALL = CELLS + 8
 WIDE = 1024
+FAR_FIRST = (4, 5, 3, 2, 6, 1, 7)
 MESH = pl.DeviceIdType.MESH
 BF = ml_dtypes.bfloat16
 
@@ -151,9 +152,9 @@
 
 
 def section_kernel(
-    start, sec, zon, mer, ut_h, pt_h, qt_h, cut, rc, nest,
+    start, sec, zon, mer, ut_h, pt_h, qt_h, cut_h, rc_h, nest_h,
     zout, sect, nestg,
-    sb, tb, zb, mb, ut, pt, qt, sh, sl, pk, pkr, lh,
+    cut, rc, nest, sb, tb, zb, mb, ut, pt, qt, sh, sl, pk, pkr, lh,
     fsend, recv, bsend, nsend, ngat, nasm,
     ld, tabs, psend, precv, lsend, lrecv, fs, fr, bs, br, n1s, n1r, n2s, n2r, osem, zsem,
 ):
@@ -179,12 +180,13 @@
     tables = [
         pltpu.make_async_copy(src, dst, tabs.at[n]) for n, (src, dst) in enumerate(((ut_h, ut), (pt_h, pt), (qt_h, qt)))
     ]
-    for copy in loads[0] + tables[:1] + loads[1] + loads[2] + tables[1:]:
+    small = [
+        pltpu.make_async_copy(src, dst, tabs.at[3 + n])
+        for n, (src, dst) in enumerate(((nest_h, nest), (rc_h.at[lat], rc), (cut_h, cut)))
+    ]
+    for copy in small + loads[0] + tables[:1] + loads[1] + loads[2] + tables[1:]:
         copy.start()
 
-    for n in range(12):
-        nsend[n : n + 1, :] = nest[n // 6, n % 6]
-    nsend[12:16, :] = jnp.zeros((4, 256), jnp.float32)
     for buf in (tb, zb, mb, sb):
         for lev in range(LEV):
             buf[lev, SEG:TALL, :] = jnp.zeros((TALL - SEG, ROWS), jnp.float32)
@@ -243,6 +245,10 @@
                 for a in range(2):
                     pkr[c, way, a] = jnp.zeros((STEP, ROWS), jnp.float32)
 
+    small[0].wait()
+    for n in range(12):
+        nsend[n : n + 1, :] = nest[n // 6, n % 6]
+    nsend[12:16, :] = jnp.zeros((4, 256), jnp.float32)
     for k in range(1, SEGS):
         copy = pltpu.make_async_remote_copy(
             src_ref=nsend, dst_ref=ngat.at[lon], send_sem=n1s.at[k], recv_sem=n1r.at[k],
@@ -252,10 +258,10 @@
         nest_copies.append(copy)
     ngat[lon] = nsend[...]
 
-    edge_row = rc[lat, 0:1, :]
-    inverse_cos = rc[lat, 1:2, :]
-    first_edge, last_edge = rc[lat, 2:3, :], rc[lat, 3:4, :]
-    end_scale = rc[lat, 4:5, :]
+    small[1].wait()
+    small[2].wait()
+    edge_row, inverse_cos = rc[0:1, :], rc[1:2, :]
+    first_edge, last_edge, end_scale = rc[2:3, :], rc[3:4, :], rc[4:5, :]
     flux_scale = jnp.where(even[:1], last_edge, first_edge)
 
     def inner(c):
@@ -386,7 +392,7 @@
                         acc = v if acc is None else jnp.where(block == j, v, acc)
                     fsend[c, 4 * h + q] = acc
             recv[c, lon] = fsend[c, lon]
-            there.append([exchange(c, k, fsend, recv, fs, fr) for k in range(1, SEGS)])
+            there.append([exchange(c, k, fsend, recv, fs, fr) for k in FAR_FIRST])
             for copy in there[c]:
                 copy.start()
             if c == 0:
@@ -431,7 +437,7 @@
             for e in range(4):
                 bsend[c, e] = evens[e] + odds[e]
                 bsend[c, e + 4] = evens[e] - odds[e]
-            back.append([exchange(c, k, bsend, zout, bs, br) for k in range(1, SEGS)])
+            back.append([exchange(c, k, bsend, zout, bs, br) for k in FAR_FIRST])
             for copy in back[c]:
                 copy.start()
             copy = pltpu.make_async_copy(bsend.at[c, lon], zout.at[c, lon], zsem.at[c])
@@ -554,9 +560,10 @@
             jax.ShapeDtypeStruct((LEV, SEG, ROWS), f32),
             jax.ShapeDtypeStruct((LEV, 128, 256), f32),
         ),
-        in_specs=[anywhere] * 7 + [vmem] * 3,
+        in_specs=[anywhere] * 10,
         out_specs=(anywhere,) * 3,
         scratch_shapes=[
+            pltpu.VMEM((BANDS, ROWS), jnp.int32), pltpu.VMEM((8, ROWS), f32), pltpu.VMEM((2, LEV, 1, 256), f32),
             field, field, field, field,
             pltpu.VMEM((2 * RANK, WIDE), bf), pltpu.VMEM((4, 256, 4 * RANK), bf), pltpu.VMEM((4, 2 * RANK, 512), bf),
             pltpu.VMEM((CHUNKS, WIDE, 256), bf), pltpu.VMEM((CHUNKS, WIDE, 256), bf),
@@ -565,7 +572,7 @@
             pltpu.VMEM((CHUNKS, SEGS, PART, ROWS), f32), pltpu.VMEM((CHUNKS, SEGS, PART, ROWS), f32),
             pltpu.VMEM((CHUNKS, SEGS, PART, ROWS), f32),
             pltpu.VMEM((16, 256), f32), pltpu.VMEM((SEGS, 16, 256), f32), pltpu.VMEM((2, LEV, SEGS, 256), f32),
-            dma((CHUNKS, 4)), dma((3,)), dma((CHUNKS, 2)), dma((CHUNKS, 2)), dma((2, 2)), dma((2, 2)),
+            dma((CHUNKS, 4)), dma((6,)), dma((CHUNKS, 2)), dma((CHUNKS, 2)), dma((2, 2)), dma((2, 2)),
             dma((CHUNKS, SEGS)), dma((CHUNKS, SEGS)), dma((CHUNKS, SEGS)), dma((CHUNKS, SEGS)),
             dma((SEGS,)), dma((SEGS,)), dma((BANDS,)), dma((BANDS,)), dma((LEV + 1,)), dma((CHUNKS,)),
         ],

time: 34.1 us -> 32.7 us (0.959)
  Pallas kernels: 33.8 us -> 32.4 us
    pallas_call x1, Pallas kernels: 30 us -> 28.6 us  [shards(): pl.pallas_call(section_kernel, out_shape=(jax.ShapeDtypeStruct((CHUNKS, S...]
where the time goes in v4:
time: 32.7 us; the launch traced here: 32.6 us
  Pallas kernels  32.4 us (99%)
    pallas_call x1, Pallas kernels, shards(): pl.pallas_call(section_kernel, out_shape=(jax.ShapeDtypeStruct((CHUNKS, S...  28.6 us
    pallas_call x1, Pallas kernels, shards(): pl.pallas_call(finish_kernel, out_shape=jax.ShapeDtypeStruct((LEV, SEG, R...  3.76 us

profile of v4, /device:TPU:1, one launch (start us, length us, event | category | flops | bytes accessed | tf_op | source)
XLA Modules:
  0.0 32.6 jit_solution(4251131110803518698)
XLA Ops:
  0.0 28.6 %shard_map.118 = (f32[3,8,40,128]{3,2,1,0:T(8,128)}, f32[6,900,128]{2,1,0:T(8,128)}, f32[6,128,256]{2,1,0:T(8,128)}) custom-call(f32[6,900,128]{2,1,0:T(8,128)} %bitcast.6, f32[6,900,128]{2,1,0:T(8,128)} %bitcast.7, f32[6,900,128]{2,1,0:T(8,128)} %bitcast.8, f32[6,900,128]{2,1,0:T(8,128)} %bitcast.9, bf16[320,1024]{1,0:T(8,128)(2,1)} %constant.10.clone.ut_h, ...), custom_call_target="tpu_custom_call" | custom-call | flops 1000000000 | bytes 16000000 | tf_op jit(solution)/shard_map/pallas_call | solution.py:556
  28.7 3.8 %shard_map.119 = f32[6,900,128]{2,1,0:T(8,128)} custom-call(s32[2,2]{1,0:T(2,128)} %corners.1, f32[3,8,40,128]{3,2,1,0:T(8,128)} %get-tuple-element.8.zin, bf16[928,512]{1,0:T(8,128)(2,1)} %constant.11.clone.eu, f32[6,900,128]{2,1,0:T(8,128)} %get-tuple-element.9.sect, f32[6,128,256]{2,1,0:T(8,128)} %get-tuple-element.10.nestg), custom_call_target="tpu_custom_call" | custom-call | flops 1000000000 | bytes 4000000 | tf_op jit(solution)/shard_map/pallas_call | solution.py:587

commit v5 on v4

--- a/solution.py
+++ b/solution.py
@@ -382,6 +382,7 @@
                 tables[0].wait()
             both = dot(ut[...], sh[c])
             y = both[:RANK] + both[RANK:] + dot(ut[:RANK, :], sl[c])
+            there.append([exchange(c, k, fsend, recv, fs, fr) for k in FAR_FIRST])
             for h in range(PAIR):
                 for q in range(4):
                     acc = None
@@ -391,10 +392,9 @@
                             v = pltpu.roll(v, (32 * (j - q)) % ROWS, 1)
                         acc = v if acc is None else jnp.where(block == j, v, acc)
                     fsend[c, 4 * h + q] = acc
+                for k, copy in zip(FAR_FIRST, there[c]):
+                    pl.when(lax.rem(lon + k, SEGS) // 4 == h)(copy.start)
             recv[c, lon] = fsend[c, lon]
-            there.append([exchange(c, k, fsend, recv, fs, fr) for k in FAR_FIRST])
-            for copy in there[c]:
-                copy.start()
             if c == 0:
                 spread_nest()
 

time: 32.7 us -> 33.1 us (1.012)
  Pallas kernels: 32.4 us -> 32.8 us
    pallas_call x1, Pallas kernels: 28.6 us -> 29.1 us  [shards(): pl.pallas_call(section_kernel, out_shape=(jax.ShapeDtypeStruct((CHUNKS, S...]
where the time goes in v5:
time: 33.1 us; the launch traced here: 33 us
  Pallas kernels  32.8 us (99%)
    pallas_call x1, Pallas kernels, shards(): pl.pallas_call(section_kernel, out_shape=(jax.ShapeDtypeStruct((CHUNKS, S...  29.1 us
    pallas_call x1, Pallas kernels, shards(): pl.pallas_call(finish_kernel, out_shape=jax.ShapeDtypeStruct((LEV, SEG, R...  3.76 us

profile of v5, /device:TPU:1, one launch (start us, length us, event | category | flops | bytes accessed | tf_op | source)
XLA Modules:
  0.0 33.0 jit_solution(4416826848387392548)
XLA Ops:
  0.0 29.1 %shard_map.118 = (f32[3,8,40,128]{3,2,1,0:T(8,128)}, f32[6,900,128]{2,1,0:T(8,128)}, f32[6,128,256]{2,1,0:T(8,128)}) custom-call(f32[6,900,128]{2,1,0:T(8,128)} %bitcast.6, f32[6,900,128]{2,1,0:T(8,128)} %bitcast.7, f32[6,900,128]{2,1,0:T(8,128)} %bitcast.8, f32[6,900,128]{2,1,0:T(8,128)} %bitcast.9, bf16[320,1024]{1,0:T(8,128)(2,1)} %constant.10.clone.ut_h, ...), custom_call_target="tpu_custom_call" | custom-call | flops 1000000000 | bytes 16000000 | tf_op jit(solution)/shard_map/pallas_call | solution.py:556
  29.1 3.8 %shard_map.119 = f32[6,900,128]{2,1,0:T(8,128)} custom-call(s32[2,2]{1,0:T(2,128)} %corners.1, f32[3,8,40,128]{3,2,1,0:T(8,128)} %get-tuple-element.8.zin, bf16[928,512]{1,0:T(8,128)(2,1)} %constant.11.clone.eu, f32[6,900,128]{2,1,0:T(8,128)} %get-tuple-element.9.sect, f32[6,128,256]{2,1,0:T(8,128)} %get-tuple-element.10.nestg), custom_call_target="tpu_custom_call" | custom-call | flops 1000000000 | bytes 4000000 | tf_op jit(solution)/shard_map/pallas_call | solution.py:587
